TPU v7x, 512 devices: a whole 4x4x16 slice. The times are simulated.
512 devices in a mesh: dp: 16 (over y, z_hi), tensor: 32 (over z_lo, x, core).
Axes of the slice: x: 4, y: 4, z: 16 (z_hi: 4, z_lo: 4; z = z_hi * 4 + z_lo), core: 2. Of those that a mesh axis runs over, the one named last changes fastest.
Arguments:
- tokens: bfloat16 [65536, 6144], P(('dp', 'tensor')), may hold values from -6 to 6
- expert_ids: int32 [65536, 2], P(('dp', 'tensor')), may hold values from 0 to 7, as said below
- slots: int32 [65536, 2], P(('dp', 'tensor')), may hold values from 0 to 128, as said below
- route_gates: float32 [65536, 2], P(('dp', 'tensor')), may hold values from 0.2 to 1
- w_gate: bfloat16 [6144, 16384], P('dp', 'tensor'), may hold values from -0.078125 to 0.078125
- w_up: bfloat16 [6144, 16384], P('dp', 'tensor'), may hold values from -0.078125 to 0.078125
- w_down: bfloat16 [16384, 6144], P('tensor', 'dp'), may hold values from -0.046875 to 0.046875
Outputs:
- mixed: bfloat16 [65536, 6144], P(('dp', 'tensor'))
Inputs may be any that keep to these rules, and one draw needn't show every extreme that they name: `expert_ids`: each token names 2 different experts; every expert is named somewhere. Each device holds 128 consecutive tokens. A route's slot is (the device's index along tensor) * 4 plus the number of earlier routes of the same device to the same expert (tokens in order, then a token's routes in order) when that number is under 4, else 128 (dropped). In every draw all 128 slots of expert 0 of some group are used and some routes are dropped.
All inputs are finite; a program needn't handle non-finite values.
Results may differ from a plain program's by a relative error of at most 0.005.
Values may be sent and summed in bfloat16 or wider, within the bound.
No kernel may reach another device: no remote copies, remote signals or barrier semaphores. Data moves between devices by JAX's collectives and lax.ppermute only.
A program may use at most 64 MiB of HBM per device.

v0:
```python
import jax
import jax.numpy as jnp
from jax import lax
from jax.sharding import PartitionSpec as P

SLOT_DEV = 4


def per_device(tokens, expert_ids, slots, route_gates, w_gate, w_up, w_down):
    slot_base = lax.axis_index("tensor") * SLOT_DEV
    local_slot = jnp.where(expert_ids == 0, slots - slot_base, SLOT_DEV)
    positions = jnp.arange(SLOT_DEV, dtype=jnp.int32)
    route_hits = (local_slot[:, :, None] == positions).astype(jnp.float32)
    placing = jnp.sum(route_hits, axis=1).astype(jnp.bfloat16)
    sending = lax.dot_general(
        placing, tokens, (((0,), (0,)), ((), ())), preferred_element_type=jnp.float32
    ).astype(jnp.bfloat16)
    slot_block = lax.all_gather(sending, "tensor", axis=0, tiled=True)
    gate_sum = jnp.dot(
        slot_block,
        lax.all_gather(w_gate, "dp", axis=0, tiled=True),
        preferred_element_type=jnp.float32,
    )
    up_sum = jnp.dot(
        slot_block,
        lax.all_gather(w_up, "dp", axis=0, tiled=True),
        preferred_element_type=jnp.float32,
    )
    hidden = (jax.nn.silu(gate_sum) * up_sum).astype(jnp.bfloat16)
    down_terms = jnp.dot(
        hidden, lax.all_gather(w_down, "dp", axis=1, tiled=True), preferred_element_type=jnp.float32
    )
    expert_out = lax.psum_scatter(down_terms, "tensor", scatter_dimension=0, tiled=True)
    mixing = jnp.sum(route_hits * route_gates[:, :, None], axis=1)
    output_rows = jnp.dot(
        mixing, expert_out, precision=lax.Precision.HIGHEST, preferred_element_type=jnp.float32
    )
    return output_rows.astype(jnp.bfloat16)


def solution(mesh):
    return jax.shard_map(
        per_device,
        mesh=mesh,
        in_specs=(
            P(("dp", "tensor"), None),
            P(("dp", "tensor"), None),
            P(("dp", "tensor"), None),
            P(("dp", "tensor"), None),
            P("dp", "tensor"),
            P("dp", "tensor"),
            P("tensor", "dp"),
        ),
        out_specs=P(("dp", "tensor"), None),
        check_vma=False,
    )
```

profile of v0, /device:TPU:1, one launch (start us, length us, event | category | flops | bytes accessed | tf_op | source)
XLA Modules:
  0.0 925.7 jit_solution(7332926750126357976)
XLA Ops:
  6.5 0.0 copy-start
  6.5 0.0 all-gather.12.cloned.1.call-start
  6.5 0.8 compare_select_fusion
  7.4 0.7 convert_reduce_fusion
  8.1 0.0 copy-done
  8.1 0.9 fusion
  9.0 0.0 all-gather.12.cloned.1.call-update
  9.0 0.0 all-gather.6.cloned.1.call-start
  9.1 0.7 all-gather.6.cloned.1.call-update
  9.8 0.0 all-gather.10.cloned.1.call-start
  9.8 0.7 all-gather.10.cloned.1.call-update
  10.5 0.0 all-gather.8.cloned.1.call-start
  10.5 0.5 all-gather.8.cloned.1.call-update
  11.1 0.0 all-reduce.3.cloned.1.call-start
  11.1 68.9 %all-gather.12.cloned.1.call-done = bf16[32,4,6144]{2,1,0:T(4,128)(2,1)} async-done(((bf16[1,4,6144]{2,1,0:T(4,128)(2,1)}), bf16[32,4,6144]{2,1,0:T(4,128)(2,1)}) %all-gather.12.cloned.1.call-update) | async-done | bytes 1572880 | tf_op jit(solution)/shard_map/all_gather | solution.py:18
  80.0 2.7 reshape.3
  82.7 176.0 %all-gather.6.cloned.1.call-done = bf16[6144,512]{1,0:T(8,128)(2,1)} async-done(((bf16[384,512]{1,0:T(8,128)(2,1)}), bf16[6144,512]{1,0:T(8,128)(2,1)}) %all-gather.6.cloned.1.call-update) | async-done | bytes 6291472 | tf_op jit(solution)/shard_map/all_gather | solution.py:21
  258.6 3.8 fusion.13
  262.4 178.8 %all-gather.10.cloned.1.call-done = bf16[512,6144]{1,0:T(8,128)(2,1)} async-done(((bf16[512,384]{1,0:T(8,128)(2,1)}), bf16[512,6144]{1,0:T(8,128)(2,1)}) %all-gather.10.cloned.1.call-update) | async-done | bytes 6291472 | tf_op jit(solution)/shard_map/all_gather | solution.py:31
  441.2 173.5 %all-gather.8.cloned.1.call-done = bf16[6144,512]{1,0:T(8,128)(2,1)} async-done(((bf16[384,512]{1,0:T(8,128)(2,1)}), bf16[6144,512]{1,0:T(8,128)(2,1)}) %all-gather.8.cloned.1.call-update) | async-done | bytes 6291472 | tf_op jit(solution)/shard_map/all_gather | solution.py:26
  614.6 8.2 fusion.2
  622.8 0.0 all-reduce.3.cloned.1.call-update
  622.8 1.3 dynamic-slice
  624.8 289.6 %all-reduce.3.cloned.1.call-done = f32[128,6144]{1,0:T(8,128)} async-done(((f32[128,6144]{1,0:T(8,128)}), f32[128,6144]{1,0:T(8,128)}) %all-reduce.3.cloned.1.call-update) | async-done | bytes 3145744
  914.4 4.7 convolution_convert_fusion
Async XLA Ops:
  6.5 1.5 copy-start
  6.5 73.4 %all-gather.12.cloned.1.call-start = ((), (), s32[]{:S(2)}) async-start(), calls=%async_computation.3 | async-start | bytes 1622016 | tf_op jit(solution)/shard_map/all_gather | solution.py:18
  9.0 249.6 %all-gather.6.cloned.1.call-start = ((), (), s32[]{:S(2)}) async-start(), calls=%async_computation | async-start | bytes 6684672 | tf_op jit(solution)/shard_map/all_gather | solution.py:21
  9.8 431.4 %all-gather.10.cloned.1.call-start = ((), (), s32[]{:S(2)}) async-start(), calls=%async_computation.2 | async-start | bytes 6684672 | tf_op jit(solution)/shard_map/all_gather | solution.py:31
  10.5 604.1 %all-gather.8.cloned.1.call-start = ((), (), s32[]{:S(2)}) async-start(), calls=%async_computation.1 | async-start | bytes 6684672 | tf_op jit(solution)/shard_map/all_gather | solution.py:26
  11.1 903.3 %all-reduce.3.cloned.1.call-start = ((), (), s32[]{:S(2)}) async-start(), calls=%async_computation.4 | async-start | bytes 6291456
Sparse Core Ops, SparseCore 0:
  9.5 70.4 all-gather.11
  83.0 175.5 all-gather.5
  261.6 179.5 all-gather.9
  444.1 170.4 all-gather.7
  623.0 291.4 all-reduce.2
where the time goes:
time: 926 us
  waiting for transfers between devices  889 us (96%)
  matrix products  17.6 us (2%)
  between operations  13.8 us (1%)
    unnamed x6, waiting for transfers between devices  292 us
    all_gather x1, waiting for transfers between devices, per_device(): lax.all_gather(w_down, 'dp', axis=1, tiled=True)  179 us
    all_gather x1, waiting for transfers between devices, per_device(): lax.all_gather(w_gate, 'dp', axis=0, tiled=True)  176 us
    all_gather x1, waiting for transfers between devices, per_device(): lax.all_gather(w_up, 'dp', axis=0, tiled=True)  173 us
    all_gather x1, waiting for transfers between devices, per_device(): slot_block = lax.all_gather(sending, 'tensor', axis=0, tiled=True)  68.9 us
  transfers between devices with their start and end apart: 5, of which 5 were waited for; matrix products, arithmetic and copies ran while one was open for 1% of the time, Pallas kernels for 0%

commit v1 on v0

v1 whole, which is shorter than its diff:
```python
import jax
import jax.numpy as jnp
from jax import lax
from jax.sharding import Mesh
from jax.sharding import PartitionSpec as P

SLOT_DEV = 4
AXES = ("y", "zh", "zl", "x", "c")
SIZES = (4, 4, 4, 4, 2)
CHUNKS = 1
XC = False
BF16, F32 = jnp.bfloat16, jnp.float32


def exchange(pieces, axis):
    return lax.all_to_all(pieces, axis, 0, 0, tiled=True)


def spread(block, axis, size):
    return exchange(jnp.broadcast_to(block[None], (size, *block.shape)), axis)


def per_device(tokens, expert_ids, slots, route_gates, w_gate, w_up, w_down):
    ny, ns, nl, nx, nc = SIZES
    d = tokens.shape[1]
    piece = d // (ny * ns)
    cols = ny * piece
    ff = w_gate.shape[1]
    part = ff // CHUNKS
    swap = [(0, 1), (1, 0)]

    stacked = []
    for k in range(CHUNKS):
        stacked += [w_gate[:, k * part : (k + 1) * part], w_up[:, k * part : (k + 1) * part]]
    in_rows = lax.all_gather(jnp.concatenate(stacked, axis=1), "y", axis=0, tiled=True)
    down_cols = lax.all_gather(w_down, "y", axis=1, tiled=True)

    slot_base = lax.axis_index(("zl", "x", "c")) * SLOT_DEV
    local_slot = jnp.where(expert_ids == 0, slots - slot_base, SLOT_DEV)
    positions = jnp.arange(SLOT_DEV, dtype=jnp.int32)
    route_hits = (local_slot[:, :, None] == positions).astype(F32)
    placing = jnp.sum(route_hits, axis=1).astype(BF16)
    mixing = jnp.sum(route_hits * route_gates[:, :, None], axis=1)
    sending = lax.dot_general(
        placing, tokens, (((0,), (0,)), ((), ())), preferred_element_type=F32
    ).astype(BF16)

    with jax.named_scope("spread_rows"):
        parts = jnp.transpose(sending.reshape(SLOT_DEV, ny, ns, piece), (2, 0, 1, 3))
        parts = parts.reshape(ns, 1, SLOT_DEV, cols)
        parts = jnp.broadcast_to(parts, (ns, nl, SLOT_DEV, cols)).reshape(ns * nl, SLOT_DEV, cols)
        rows = exchange(parts, ("zh", "zl")).reshape(ns * nl * SLOT_DEV, cols)
        rows = spread(rows, "x", nx)
        few = nl * SLOT_DEV
        rows = jnp.transpose(rows.reshape(nx, ns, few, cols), (1, 0, 2, 3))
        rows = rows.reshape(ns, nx * few, cols)
        other = lax.ppermute(rows, "c", swap)
        block = jnp.concatenate([rows, other], axis=1)
        many = nc * nx * few
        block = block.reshape(ns * many, cols)

    with jax.named_scope("expert"):
        sums = []
        for k in range(CHUNKS):
            both = jnp.dot(
                block, in_rows[:, 2 * part * k : 2 * part * (k + 1)], preferred_element_type=F32
            ).astype(BF16)
            sums.append(exchange(both.reshape(ns, many, 2 * part), "zh"))
        total = None
        for k in range(CHUNKS):
            both = jnp.sum(sums[k].astype(F32), axis=0)
            hidden = (jax.nn.silu(both[:, :part]) * both[:, part:]).astype(BF16)
            hidden = spread(hidden, "zh", ns)
            if XC:
                hidden = jnp.transpose(hidden.reshape(ns, nc, nx, few, part), (2, 1, 0, 3, 4))
            else:
                hidden = jnp.transpose(hidden.reshape(ns, nc, nx, few, part), (1, 2, 0, 3, 4))
            hidden = hidden.reshape(ns * many, part)
            terms = jnp.dot(
                hidden, down_cols[part * k : part * (k + 1)], preferred_element_type=F32
            )
            total = terms if total is None else total + terms

    with jax.named_scope("collect"):
        if XC:
            mine = lax.axis_index("c")
            terms = total.reshape(nx, 2, ns * few, cols)
            terms = jnp.where(mine == 0, terms, terms[:, ::-1])
            terms = terms.astype(BF16).reshape(nx * 2, ns * few, cols)
            terms = exchange(terms, ("x", "c"))
        else:
            terms = total.reshape(nc, nx * ns * few, cols)
            terms = terms[0] + lax.ppermute(terms[1], "c", swap)
            terms = exchange(terms.astype(BF16).reshape(nx, ns * few, cols), "x")
        terms = jnp.sum(terms.astype(F32), axis=0)
        terms = exchange(terms.reshape(ns * nl, SLOT_DEV, cols), ("zh", "zl"))
        terms = jnp.sum(terms.reshape(ns, nl, SLOT_DEV, cols), axis=1)

    with jax.named_scope("mix"):
        terms = jnp.transpose(terms.reshape(ns, SLOT_DEV, ny, piece), (1, 2, 0, 3))
        expert_out = terms.reshape(SLOT_DEV, d)
        out = mixing[:, 0:1] * expert_out[0:1]
        for s in range(1, SLOT_DEV):
            out = out + mixing[:, s : s + 1] * expert_out[s : s + 1]
    return out.astype(BF16)


def solution(mesh):
    fine = Mesh(mesh.devices.reshape(SIZES), AXES)
    rows = P(AXES, None)
    dp, tensor = AXES[:2], AXES[2:]
    return jax.shard_map(
        per_device,
        mesh=fine,
        in_specs=(rows, rows, rows, rows, P(dp, tensor), P(dp, tensor), P(tensor, dp)),
        out_specs=rows,
        check_vma=False,
    )
```

time: 926 us -> 225 us (0.24)
  the two profiles are of different devices: /device:TPU:1 before, /device:TPU:64 now
where the time goes in v1:
time: 225 us
  blocking collectives  95.6 us (42%)
  waiting for transfers between devices  82.9 us (37%)
  starting transfers between devices  18.5 us (8%)
  between operations  13.6 us (6%)
  matrix products  7.41 us (3%)
  other arithmetic  5.13 us (2%)
    all_to_all x4, blocking collectives, exchange(): return lax.all_to_all(pieces, axis, 0, 0, tiled=True)  95.6 us
    all_to_all x2, waiting for transfers between devices, exchange(): return lax.all_to_all(pieces, axis, 0, 0, tiled=True)  74.3 us
    all_to_all x2, starting transfers between devices, exchange(): return lax.all_to_all(pieces, axis, 0, 0, tiled=True)  14.6 us
    dot_general x1, matrix products, per_device(): jnp.dot(block, in_rows[:, 2 * part * k:2 * part * (k + 1)], preferred_ele...  4.71 us
  transfers between devices with their start and end apart: 6, of which 5 were waited for; matrix products, arithmetic and copies ran while one was open for 0% of the time, Pallas kernels for 0%

profile of v1, /device:TPU:64, one launch (start us, length us, event | category | flops | bytes accessed | tf_op | source)
XLA Modules:
  0.0 224.7 jit_solution(11744154205629807987)
XLA Ops:
  6.5 0.0 copy-start
  6.5 0.0 copy-start.1
  6.5 0.0 copy-start.2
  6.5 0.0 copy-start.3
  6.5 0.0 all-gather.3.cloned.1.call-start
  6.6 2.2 pad_maximum_fusion.1
  8.8 0.0 all-gather.3.cloned.1.call-update
  8.8 0.0 copy-done.1
  8.8 0.0 copy-done.2
  8.8 0.0 copy-done.3
  8.9 0.0 copy-done
  8.9 0.3 convolution_convert_fusion
  9.3 0.1 broadcast_in_dim.29
  9.4 30.9 %all_to_all.30 = bf16[16,4,1536]{2,1,0:T(4,128)(2,1)S(1)} all-to-all(bf16[16,4,1536]{2,1,0:T(4,128)(2,1)S(1)} %bitcast.40), channel_id=1, replica_groups=mesh['y'=4,'zh'=4,'zl'=4,'x'=4,'c'=2] {'zh','zl'}, dimensions={0} | all-to-all | bytes 393216 | tf_op jit(solution)/shard_map/spread_rows/all_to_all | solution.py:16
  40.2 0.1 broadcast_in_dim.30
  40.3 0.1 broadcast_in_dim.31
  40.4 13.5 %all_to_all.31 = bf16[4,64,1536]{2,1,0:T(8,128)(2,1)S(1)} all-to-all(bf16[4,64,1536]{2,1,0:T(8,128)(2,1)S(1)} %broadcast_in_dim.31), channel_id=1, replica_groups=mesh['y'=4,'zh'=4,'zl'=4,'x'=4,'c'=2] {'x'}, dimensions={0} | all-to-all | bytes 1572864 | tf_op jit(solution)/shard_map/spread_rows/all_to_all | solution.py:16
  53.9 0.1 copy.23
  54.0 1.9 collective-permute-start
  55.9 2.3 %collective-permute-done = bf16[4,64,1536]{2,1,0:T(8,128)(2,1)S(1)} collective-permute-done((bf16[4,64,1536]{2,1,0:T(8,128)(2,1)S(1)}, bf16[4,64,1536]{2,1,0:T(8,128)(2,1)S(1)}, u32[]{:S(2)}, u32[]{:S(2)}) %collective-permute-start) | collective-permute-done | bytes 786464 | tf_op jit(solution)/shard_map/spread_rows/ppermute | solution.py:57
  58.1 0.1 pad_maximum_fusion
  58.2 2.3 %all-gather.3.cloned.1.call-done = bf16[1536,1024]{1,0:T(8,128)(2,1)} async-done(((bf16[384,1024]{1,0:T(8,128)(2,1)}), bf16[1536,1024]{1,0:T(8,128)(2,1)}) %all-gather.3.cloned.1.call-update) | async-done | bytes 3145744 | tf_op jit(solution)/shard_map/all_gather | solution.py:35
  60.5 4.7 %convolution_convert_fusion.1 = bf16[512,1024]{1,0:T(8,128)(2,1)} fusion(bf16[512,1536]{1,0:T(8,128)(2,1)S(1)} %bitcast.38, bf16[1536,1024]{1,0:T(8,128)(2,1)} %all-gather.3.cloned.1.call-done), kind=kOutput, calls=%fused_computation.7 | convolution fusion | flops 1611137024 | bytes 5767168 | tf_op jit(solution)/shard_map/expert/dot_general | solution.py:65
  65.2 10.4 %all-to-all-start.2 = ((bf16[4,128,1024]{2,1,0:T(8,128)(2,1)}), bf16[4,128,1024]{2,1,0:T(8,128)(2,1)S(1)}, u32[]{:S(2)}, u32[]{:S(2)}) async-start(bf16[4,128,1024]{2,1,0:T(8,128)(2,1)} %bitcast.39), calls=%async_computation.2 | async-start | bytes 2097152 | tf_op jit(solution)/shard_map/expert/all_to_all | solution.py:16
  75.6 0.0 all-gather.5.cloned.1.call-start
  75.6 0.7 all-gather.5.cloned.1.call-update
  76.3 51.8 %all-to-all-done.2 = bf16[4,128,1024]{2,1,0:T(8,128)(2,1)S(1)} async-done(((bf16[4,128,1024]{2,1,0:T(8,128)(2,1)}), bf16[4,128,1024]{2,1,0:T(8,128)(2,1)S(1)}, u32[]{:S(2)}, u32[]{:S(2)}) %all-to-all-start.2) | async-done | bytes 1048608 | tf_op jit(solution)/shard_map/expert/all_to_all | solution.py:16
  128.1 0.2 convert_reduce_fusion
  128.3 0.1 fusion.1
  128.5 34.6 %all_to_all.32 = bf16[4,128,512]{2,1,0:T(8,128)(2,1)S(1)} all-to-all(bf16[4,128,512]{2,1,0:T(8,128)(2,1)S(1)} %broadcast_in_dim.32), channel_id=1, replica_groups=mesh['y'=4,'zh'=4,'zl'=4,'x'=4,'c'=2] {'zh'}, dimensions={0} | all-to-all | bytes 1048576 | tf_op jit(solution)/shard_map/expert/all_to_all | solution.py:16
  163.1 0.0 all-gather.5.cloned.1.call-done
  163.1 2.4 %fusion.4 = f32[512,1536]{1,0:T(8,128)S(1)} fusion(bf16[512,512]{1,0:T(8,128)(2,1)S(1)} %bitcast.36, bf16[512,1536]{1,0:T(8,128)(2,1)} %all-gather.5.cloned.1.call-done), kind=kOutput, calls=%fused_computation.23 | convolution fusion | flops 805306368 | bytes 5242880 | tf_op jit(solution)/shard_map/expert/dot_general | solution.py:79
  165.5 0.1 slice.57
  165.6 1.9 collective-permute-start.1
  167.5 3.4 %collective-permute-done.1 = f32[256,1536]{1,0:T(8,128)S(1)} collective-permute-done((f32[256,1536]{1,0:T(8,128)S(1)}, f32[256,1536]{1,0:T(8,128)S(1)}, u32[]{:S(2)}, u32[]{:S(2)}) %collective-permute-start.1) | collective-permute-done | bytes 1572896 | tf_op jit(solution)/shard_map/collect/ppermute | solution.py:93
  170.9 0.2 fusion
  171.2 16.6 %all_to_all.33 = bf16[4,64,1536]{2,1,0:T(8,128)(2,1)S(1)} all-to-all(bf16[4,64,1536]{2,1,0:T(8,128)(2,1)S(1)} %bitcast.35), channel_id=1, replica_groups=mesh['y'=4,'zh'=4,'zl'=4,'x'=4,'c'=2] {'x'}, dimensions={0} | all-to-all | bytes 1572864 | tf_op jit(solution)/shard_map/collect/all_to_all | solution.py:16
  187.8 0.1 convert_reduce_fusion.1
  187.9 0.9 reshape.66
  188.8 4.2 %all-to-all-start.5 = ((f32[16,4,1536]{2,1,0:T(4,128)}), f32[16,4,1536]{2,1,0:T(4,128)S(1)}, u32[]{:S(2)}, u32[]{:S(2)}) async-start(f32[16,4,1536]{2,1,0:T(4,128)} %reshape.66), calls=%async_computation.5 | async-start | bytes 786432 | tf_op jit(solution)/shard_map/collect/all_to_all | solution.py:16
  193.0 22.4 %all-to-all-done.5 = f32[16,4,1536]{2,1,0:T(4,128)S(1)} async-done(((f32[16,4,1536]{2,1,0:T(4,128)}), f32[16,4,1536]{2,1,0:T(4,128)S(1)}, u32[]{:S(2)}, u32[]{:S(2)}) %all-to-all-start.5) | async-done | bytes 393248 | tf_op jit(solution)/shard_map/collect/all_to_all | solution.py:16
  215.4 0.1 bitcast_reduce_fusion
  215.5 0.1 reshape.68
  215.7 2.1 add_convert_fusion
  (17 shorter events, 0.3 us)
Async XLA Ops:
  6.5 2.3 %copy-start = (bf16[128,6144]{1,0:T(8,128)(2,1)S(1)}, bf16[128,6144]{1,0:T(8,128)(2,1)}, u32[]{:S(2)}) copy-start(bf16[128,6144]{1,0:T(8,128)(2,1)} %param.7) | copy-start | bytes 4718596
  6.5 2.3 %copy-start.1 = (s32[128,2]{0,1:T(2,128)S(1)}, s32[128,2]{0,1:T(2,128)}, u32[]{:S(2)}) copy-start(s32[128,2]{0,1:T(2,128)} %param.8) | copy-start | bytes 3076
  6.5 2.3 %copy-start.2 = (s32[128,2]{0,1:T(2,128)S(1)}, s32[128,2]{0,1:T(2,128)}, u32[]{:S(2)}) copy-start(s32[128,2]{0,1:T(2,128)} %param.9) | copy-start | bytes 3076
  6.5 2.3 %copy-start.3 = (f32[128,2]{0,1:T(2,128)S(1)}, f32[128,2]{0,1:T(2,128)}, u32[]{:S(2)}) copy-start(f32[128,2]{0,1:T(2,128)} %param.10) | copy-start | bytes 3076
  6.5 54.0 %all-gather.3.cloned.1.call-start = ((), (), s32[]{:S(2)}) async-start(), calls=%async_computation.6 | async-start | bytes 3932160 | tf_op jit(solution)/shard_map/all_gather | solution.py:35
  54.0 4.2 %collective-permute-start = (bf16[4,64,1536]{2,1,0:T(8,128)(2,1)S(1)}, bf16[4,64,1536]{2,1,0:T(8,128)(2,1)S(1)}, u32[]{:S(2)}, u32[]{:S(2)}) collective-permute-start(bf16[4,64,1536]{2,1,0:T(8,128)(2,1)S(1)} %bitcast.33), channel_id=1, source_target_pairs={{0,1},{1,0},{2,3},{3,2},{4,5},{5,4},{6,7},{7,6},{8,9},{9,8},{10,11... | collective-permute-start | bytes 2359304 | tf_op jit(solution)/shard_map/spread_rows/ppermute | solution.py:57
  65.2 62.9 %all-to-all-start.2 = ((bf16[4,128,1024]{2,1,0:T(8,128)(2,1)}), bf16[4,128,1024]{2,1,0:T(8,128)(2,1)S(1)}, u32[]{:S(2)}, u32[]{:S(2)}) async-start(bf16[4,128,1024]{2,1,0:T(8,128)(2,1)} %bitcast.39), calls=%async_computation.2 | async-start | bytes 2097152 | tf_op jit(solution)/shard_map/expert/all_to_all | solution.py:16
  75.6 87.5 %all-gather.5.cloned.1.call-start = ((), (), s32[]{:S(2)}) async-start(), calls=%async_computation.7 | async-start | bytes 1966080 | tf_op jit(solution)/shard_map/all_gather | solution.py:36
  165.6 5.3 %collective-permute-start.1 = (f32[256,1536]{1,0:T(8,128)S(1)}, f32[256,1536]{1,0:T(8,128)S(1)}, u32[]{:S(2)}, u32[]{:S(2)}) collective-permute-start(f32[256,1536]{1,0:T(8,128)S(1)} %slice.57), channel_id=1, source_target_pairs={{0,1},{1,0},{2,3},{3,2},{4,5},{5,4},{6,7},{7,6},{8,9},{9,8},{10,11... | collective-permute-start | bytes 4718600 | tf_op jit(solution)/shard_map/collect/ppermute | solution.py:93
  188.8 26.7 %all-to-all-start.5 = ((f32[16,4,1536]{2,1,0:T(4,128)}), f32[16,4,1536]{2,1,0:T(4,128)S(1)}, u32[]{:S(2)}, u32[]{:S(2)}) async-start(f32[16,4,1536]{2,1,0:T(4,128)} %reshape.66), calls=%async_computation.5 | async-start | bytes 786432 | tf_op jit(solution)/shard_map/collect/all_to_all | solution.py:16
Sparse Core Ops, SparseCore 0:
  9.5 50.9 all-gather.2
  78.5 36.0 all-gather.4

commit v2 on v1

--- a/solution.py
+++ b/solution.py
@@ -7,7 +7,8 @@
 SLOT_DEV = 4
 AXES = ("y", "zh", "zl", "x", "c")
 SIZES = (4, 4, 4, 4, 2)
-CHUNKS = 1
+CHUNKS = 2
+AG = "pp"
 XC = False
 BF16, F32 = jnp.bfloat16, jnp.float32
 
@@ -18,6 +19,10 @@
 
 def spread(block, axis, size):
     return exchange(jnp.broadcast_to(block[None], (size, *block.shape)), axis)
+
+
+def send(block, axis, size, steps):
+    return lax.ppermute(block, axis, [(i, (i + steps) % size) for i in range(size)])
 
 
 def per_device(tokens, expert_ids, slots, route_gates, w_gate, w_up, w_down):
@@ -32,7 +37,10 @@
     stacked = []
     for k in range(CHUNKS):
         stacked += [w_gate[:, k * part : (k + 1) * part], w_up[:, k * part : (k + 1) * part]]
-    in_rows = lax.all_gather(jnp.concatenate(stacked, axis=1), "y", axis=0, tiled=True)
+    in_rows = [
+        lax.all_gather(jnp.concatenate(stacked[2 * k : 2 * k + 2], axis=1), "y", axis=0, tiled=True)
+        for k in range(CHUNKS)
+    ]
     down_cols = lax.all_gather(w_down, "y", axis=1, tiled=True)
 
     slot_base = lax.axis_index(("zl", "x", "c")) * SLOT_DEV
@@ -60,26 +68,33 @@
         block = block.reshape(ns * many, cols)
 
     with jax.named_scope("expert"):
-        sums = []
-        for k in range(CHUNKS):
-            both = jnp.dot(
-                block, in_rows[:, 2 * part * k : 2 * part * (k + 1)], preferred_element_type=F32
-            ).astype(BF16)
-            sums.append(exchange(both.reshape(ns, many, 2 * part), "zh"))
-        total = None
-        for k in range(CHUNKS):
-            both = jnp.sum(sums[k].astype(F32), axis=0)
+        zh = lax.axis_index("zh")
+        block = block.reshape(ns, many, cols)
+
+        order = sorted(range(1, ns), key=lambda k: -min(k, ns - k))
+        gathered = []
+        for h in range(CHUNKS):
+
+            def product(k):
+                picked = lax.dynamic_index_in_dim(block, (zh + k) % ns, 0, keepdims=False)
+                return jnp.dot(picked, in_rows[h], preferred_element_type=F32)
+
+            arrived = [send(product(k).astype(BF16), "zh", ns, k) for k in order]
+            both = product(0)
+            for term in arrived:
+                both = both + term.astype(F32)
             hidden = (jax.nn.silu(both[:, :part]) * both[:, part:]).astype(BF16)
+            if AG == "pp":
+                got = {k: send(hidden, "zh", ns, -k) for k in order}
+                got[0] = hidden
+                gathered.append(jnp.stack([got[k] for k in range(ns)]))
+            else:
+                gathered.append(hidden)
+        hidden = jnp.concatenate(gathered, axis=-1)
+        if AG != "pp":
             hidden = spread(hidden, "zh", ns)
-            if XC:
-                hidden = jnp.transpose(hidden.reshape(ns, nc, nx, few, part), (2, 1, 0, 3, 4))
-            else:
-                hidden = jnp.transpose(hidden.reshape(ns, nc, nx, few, part), (1, 2, 0, 3, 4))
-            hidden = hidden.reshape(ns * many, part)
-            terms = jnp.dot(
-                hidden, down_cols[part * k : part * (k + 1)], preferred_element_type=F32
-            )
-            total = terms if total is None else total + terms
+        hidden = jnp.transpose(hidden.reshape(ns, nc, nx, few, ff), (1, 2, 0, 3, 4))
+        total = jnp.dot(hidden.reshape(ns * many, ff), down_cols, preferred_element_type=F32)
 
     with jax.named_scope("collect"):
         if XC:
@@ -93,7 +108,11 @@
             terms = terms[0] + lax.ppermute(terms[1], "c", swap)
             terms = exchange(terms.astype(BF16).reshape(nx, ns * few, cols), "x")
         terms = jnp.sum(terms.astype(F32), axis=0)
-        terms = exchange(terms.reshape(ns * nl, SLOT_DEV, cols), ("zh", "zl"))
+        terms = terms.reshape(ns, nl, SLOT_DEV, cols)
+        terms = jnp.concatenate([terms, terms[:-1]], axis=0)
+        terms = lax.dynamic_slice_in_dim(terms, (ns - zh) % ns, ns, 0)
+        terms = terms.astype(BF16).reshape(ns * nl, SLOT_DEV, cols)
+        terms = exchange(terms, ("zh", "zl")).astype(F32)
         terms = jnp.sum(terms.reshape(ns, nl, SLOT_DEV, cols), axis=1)
 
     with jax.named_scope("mix"):

time: 225 us -> 216 us (0.960)
  the two profiles are of different devices: /device:TPU:64 before, /device:TPU:32 now
where the time goes in v2:
time: 216 us; the launch traced here: 215 us
  starting transfers between devices  88.3 us (41%)
  waiting for transfers between devices  47.1 us (22%)
  blocking collectives  46.7 us (22%)
  between operations  13.7 us (6%)
  matrix products  10.8 us (5%)
  other arithmetic  6.13 us (3%)
    ppermute x12, starting transfers between devices, send(): lax.ppermute(block, axis, [(i, (i + steps) % size) for i in range(size)])  70.8 us
    all_to_all x2, blocking collectives, exchange(): return lax.all_to_all(pieces, axis, 0, 0, tiled=True)  46.7 us
    all_to_all x2, waiting for transfers between devices, exchange(): return lax.all_to_all(pieces, axis, 0, 0, tiled=True)  28.6 us
    all_to_all x2, starting transfers between devices, exchange(): return lax.all_to_all(pieces, axis, 0, 0, tiled=True)  13.6 us
    ppermute x12, waiting for transfers between devices, send(): lax.ppermute(block, axis, [(i, (i + steps) % size) for i in range(size)])  9.56 us
    dot_general x8, matrix products, product(): return jnp.dot(picked, in_rows[h], preferred_element_type=F32)  8.06 us
  transfers between devices with their start and end apart: 19, of which 7 were waited for; matrix products, arithmetic and copies ran while one was open for 5% of the time, Pallas kernels for 0%

profile of v2, /device:TPU:32, one launch (start us, length us, event | category | flops | bytes accessed | tf_op | source)
XLA Modules:
  0.0 214.9 jit_solution(8115822432704298008)
XLA Ops:
  6.5 1.4 fusion.26
  8.0 0.8 pad_maximum_fusion
  8.8 0.8 pad_maximum_fusion.1
  9.7 0.3 convolution_convert_fusion
  10.2 0.1 broadcast_in_dim.23
  10.2 30.8 %all_to_all.20 = bf16[16,4,1536]{2,1,0:T(4,128)(2,1)S(1)} all-to-all(bf16[16,4,1536]{2,1,0:T(4,128)(2,1)S(1)} %bitcast.76), channel_id=1, replica_groups=mesh['y'=4,'zh'=4,'zl'=4,'x'=4,'c'=2] {'zh','zl'}, dimensions={0} | all-to-all | bytes 393216 | tf_op jit(solution)/shard_map/spread_rows/all_to_all | solution.py:17
  41.1 0.1 broadcast_in_dim.25
  41.2 15.9 %all_to_all.21 = bf16[4,64,1536]{2,1,0:T(8,128)(2,1)S(1)} all-to-all(bf16[4,64,1536]{2,1,0:T(8,128)(2,1)S(1)} %broadcast_in_dim.25), channel_id=1, replica_groups=mesh['y'=4,'zh'=4,'zl'=4,'x'=4,'c'=2] {'x'}, dimensions={0} | all-to-all | bytes 1572864 | tf_op jit(solution)/shard_map/spread_rows/all_to_all | solution.py:17
  57.1 1.9 collective-permute-start
  59.1 2.2 %collective-permute-done = bf16[4,64,1536]{2,1,0:T(8,128)(2,1)S(1)} collective-permute-done((bf16[4,64,1536]{2,1,0:T(8,128)(2,1)S(1)}, bf16[4,64,1536]{2,1,0:T(8,128)(2,1)S(1)}, u32[]{:S(2)}, u32[]{:S(2)}) %collective-permute-start) | collective-permute-done | bytes 786464 | tf_op jit(solution)/shard_map/spread_rows/ppermute | solution.py:65
  61.3 2.6 %convolution_convert_fusion.6 = bf16[128,512]{1,0:T(8,128)(2,1)} fusion(bf16[1536,512]{1,0:T(8,128)(2,1)} %all-gather.4.cloned.1.call-done, s32[]{:T(128)S(6)} %select_n.59, bf16[4,64,1536]{2,1,0:T(8,128)(2,1)S(1)} %bitcast.65, bf16[4,64,1536]{2,1,0:T(8,128)(2,1)S(1)} %collective-permute-done), kind=kOutput, calls=%fused_computation.24 | convolution fusion | flops 202178560 | bytes 3276804 | tf_op jit(solution)/shard_map/expert/dot_general | solution.py:80
  63.8 5.2 %collective-permute-start.1 = (bf16[128,512]{1,0:T(8,128)(2,1)}, bf16[128,512]{1,0:T(8,128)(2,1)S(1)}, u32[]{:S(2)}, u32[]{:S(2)}) collective-permute-start(bf16[128,512]{1,0:T(8,128)(2,1)} %convolution_convert_fusion.6), channel_id=1, source_target_pairs={{0,64},{32,96},{64,0},{96,32},{1,65},{33,97},{65,1},{97,33},{2,66}... | collective-permute-start | bytes 393224 | tf_op jit(solution)/shard_map/expert/ppermute | solution.py:25
  69.1 1.0 convolution_convert_fusion.5
  70.1 6.2 %collective-permute-start.2 = (bf16[128,512]{1,0:T(8,128)(2,1)}, bf16[128,512]{1,0:T(8,128)(2,1)S(1)}, u32[]{:S(2)}, u32[]{:S(2)}) collective-permute-start(bf16[128,512]{1,0:T(8,128)(2,1)} %convolution_convert_fusion.5), channel_id=1, source_target_pairs={{0,32},{32,64},{64,96},{96,0},{1,33},{33,65},{65,97},{97,1},{2,34}... | collective-permute-start | bytes 393224 | tf_op jit(solution)/shard_map/expert/ppermute | solution.py:25
  76.3 1.0 convolution_convert_fusion.4
  77.3 3.6 %collective-permute-start.3 = (bf16[128,512]{1,0:T(8,128)(2,1)}, bf16[128,512]{1,0:T(8,128)(2,1)S(1)}, u32[]{:S(2)}, u32[]{:S(2)}) collective-permute-start(bf16[128,512]{1,0:T(8,128)(2,1)} %convolution_convert_fusion.4), channel_id=1, source_target_pairs={{0,96},{32,0},{64,32},{96,64},{1,97},{33,1},{65,33},{97,65},{2,98}... | collective-permute-start | bytes 393224 | tf_op jit(solution)/shard_map/expert/ppermute | solution.py:25
  80.9 3.4 %all-gather.6.cloned.1.call-done = bf16[1536,512]{1,0:T(8,128)(2,1)} async-done(((bf16[384,512]{1,0:T(8,128)(2,1)}), bf16[1536,512]{1,0:T(8,128)(2,1)}) %all-gather.6.cloned.1.call-update) | async-done | bytes 1572880 | tf_op jit(solution)/shard_map/all_gather | solution.py:41
  84.3 1.9 convolution_convert_fusion.3
  86.2 11.9 %collective-permute-start.7 = (bf16[128,512]{1,0:T(8,128)(2,1)S(1)}, bf16[128,512]{1,0:T(8,128)(2,1)S(1)}, u32[]{:S(2)}, u32[]{:S(2)}) collective-permute-start(bf16[128,512]{1,0:T(8,128)(2,1)S(1)} %convolution_convert_fusion.3), channel_id=1, source_target_pairs={{0,64},{32,96},{64,0},{96,32},{1,65},{33,97},{65,1},{97,33},{2,66}... | collective-permute-start | bytes 393224 | tf_op jit(solution)/shard_map/expert/ppermute | solution.py:25
  98.2 0.4 convolution_convert_fusion.2
  98.5 3.0 %collective-permute-start.8 = (bf16[128,512]{1,0:T(8,128)(2,1)S(1)}, bf16[128,512]{1,0:T(8,128)(2,1)S(1)}, u32[]{:S(2)}, u32[]{:S(2)}) collective-permute-start(bf16[128,512]{1,0:T(8,128)(2,1)S(1)} %convolution_convert_fusion.2), channel_id=1, source_target_pairs={{0,32},{32,64},{64,96},{96,0},{1,33},{33,65},{65,97},{97,1},{2,34}... | collective-permute-start | bytes 393224 | tf_op jit(solution)/shard_map/expert/ppermute | solution.py:25
  101.5 0.4 convolution_convert_fusion.1
  101.9 6.9 %collective-permute-start.9 = (bf16[128,512]{1,0:T(8,128)(2,1)S(1)}, bf16[128,512]{1,0:T(8,128)(2,1)S(1)}, u32[]{:S(2)}, u32[]{:S(2)}) collective-permute-start(bf16[128,512]{1,0:T(8,128)(2,1)S(1)} %convolution_convert_fusion.1), channel_id=1, source_target_pairs={{0,96},{32,0},{64,32},{96,64},{1,97},{33,1},{65,33},{97,65},{2,98}... | collective-permute-start | bytes 393224 | tf_op jit(solution)/shard_map/expert/ppermute | solution.py:25
  108.9 0.4 fusion.4
  109.3 3.0 %collective-permute-start.4 = (bf16[128,256]{1,0:T(8,128)(2,1)S(1)}, bf16[128,256]{1,0:T(8,128)(2,1)S(1)}, u32[]{:S(2)}, u32[]{:S(2)}) collective-permute-start(bf16[128,256]{1,0:T(8,128)(2,1)S(1)} %fusion.16), channel_id=1, source_target_pairs={{0,96},{32,0},{64,32},{96,64},{1,97},{33,1},{65,33},{97,65},{2,98}... | collective-permute-start | bytes 196616 | tf_op jit(solution)/shard_map/expert/ppermute | solution.py:25
  112.3 7.1 %collective-permute-start.5 = (bf16[128,256]{1,0:T(8,128)(2,1)S(1)}, bf16[128,256]{1,0:T(8,128)(2,1)S(1)}, u32[]{:S(2)}, u32[]{:S(2)}) collective-permute-start(bf16[128,256]{1,0:T(8,128)(2,1)S(1)} %fusion.16), channel_id=1, source_target_pairs={{0,64},{32,96},{64,0},{96,32},{1,65},{33,97},{65,1},{97,33},{2,66}... | collective-permute-start | bytes 196616 | tf_op jit(solution)/shard_map/expert/ppermute | solution.py:25
  119.5 2.3 %collective-permute-start.6 = (bf16[128,256]{1,0:T(8,128)(2,1)S(1)}, bf16[128,256]{1,0:T(8,128)(2,1)S(1)}, u32[]{:S(2)}, u32[]{:S(2)}) collective-permute-start(bf16[128,256]{1,0:T(8,128)(2,1)S(1)} %fusion.16), channel_id=1, source_target_pairs={{0,32},{32,64},{64,96},{96,0},{1,33},{33,65},{65,97},{97,1},{2,34}... | collective-permute-start | bytes 196616 | tf_op jit(solution)/shard_map/expert/ppermute | solution.py:25
  121.8 0.4 fusion.2
  122.3 7.5 %collective-permute-start.10 = (bf16[128,256]{1,0:T(8,128)(2,1)S(1)}, bf16[128,256]{1,0:T(8,128)(2,1)S(1)}, u32[]{:S(2)}, u32[]{:S(2)}) collective-permute-start(bf16[128,256]{1,0:T(8,128)(2,1)S(1)} %fusion.15), channel_id=1, source_target_pairs={{0,96},{32,0},{64,32},{96,64},{1,97},{33,1},{65,33},{97,65},{2,98}... | collective-permute-start | bytes 196616 | tf_op jit(solution)/shard_map/expert/ppermute | solution.py:25
  129.8 7.4 %collective-permute-start.11 = (bf16[128,256]{1,0:T(8,128)(2,1)S(1)}, bf16[128,256]{1,0:T(8,128)(2,1)S(1)}, u32[]{:S(2)}, u32[]{:S(2)}) collective-permute-start(bf16[128,256]{1,0:T(8,128)(2,1)S(1)} %fusion.15), channel_id=1, source_target_pairs={{0,64},{32,96},{64,0},{96,32},{1,65},{33,97},{65,1},{97,33},{2,66}... | collective-permute-start | bytes 196616 | tf_op jit(solution)/shard_map/expert/ppermute | solution.py:25
  137.2 6.7 %collective-permute-start.12 = (bf16[128,256]{1,0:T(8,128)(2,1)S(1)}, bf16[128,256]{1,0:T(8,128)(2,1)S(1)}, u32[]{:S(2)}, u32[]{:S(2)}) collective-permute-start(bf16[128,256]{1,0:T(8,128)(2,1)S(1)} %fusion.15), channel_id=1, source_target_pairs={{0,32},{32,64},{64,96},{96,0},{1,33},{33,65},{65,97},{97,1},{2,34}... | collective-permute-start | bytes 196616 | tf_op jit(solution)/shard_map/expert/ppermute | solution.py:25
  144.1 1.8 collective-permute-done.11
  145.9 7.7 %collective-permute-done.12 = bf16[128,256]{1,0:T(8,128)(2,1)S(1)} collective-permute-done((bf16[128,256]{1,0:T(8,128)(2,1)S(1)}, bf16[128,256]{1,0:T(8,128)(2,1)S(1)}, u32[]{:S(2)}, u32[]{:S(2)}) %collective-permute-start.12) | collective-permute-done | bytes 65568 | tf_op jit(solution)/shard_map/expert/ppermute | solution.py:25
  153.7 2.4 %fusion.29 = f32[512,1536]{1,0:T(8,128)S(1)} fusion(bf16[512,512]{1,0:T(8,128)(2,1)S(1)} %bitcast.74, bf16[512,1536]{1,0:T(8,128)(2,1)} %all-gather.8.cloned.1.call-done), kind=kOutput, calls=%fused_computation.58 | convolution fusion | flops 805306368 | bytes 5242880 | tf_op jit(solution)/shard_map/expert/dot_general | solution.py:97
  156.1 0.1 slice.91
  156.2 1.9 collective-permute-start.13
  158.1 3.4 %collective-permute-done.13 = f32[256,1536]{1,0:T(8,128)S(1)} collective-permute-done((f32[256,1536]{1,0:T(8,128)S(1)}, f32[256,1536]{1,0:T(8,128)S(1)}, u32[]{:S(2)}, u32[]{:S(2)}) %collective-permute-start.13) | collective-permute-done | bytes 1572896 | tf_op jit(solution)/shard_map/collect/ppermute | solution.py:108
  161.5 1.1 fusion
  162.6 4.1 %all-to-all-start.2 = ((bf16[4,64,1536]{2,1,0:T(8,128)(2,1)}), bf16[4,64,1536]{2,1,0:T(8,128)(2,1)S(1)}, u32[]{:S(2)}, u32[]{:S(2)}) async-start(bf16[4,64,1536]{2,1,0:T(8,128)(2,1)} %bitcast.21), calls=%async_computation.2 | async-start | bytes 1572864 | tf_op jit(solution)/shard_map/collect/all_to_all | solution.py:17
  166.7 12.6 %all-to-all-done.2 = bf16[4,64,1536]{2,1,0:T(8,128)(2,1)S(1)} async-done(((bf16[4,64,1536]{2,1,0:T(8,128)(2,1)}), bf16[4,64,1536]{2,1,0:T(8,128)(2,1)S(1)}, u32[]{:S(2)}, u32[]{:S(2)}) %all-to-all-start.2) | async-done | bytes 786464 | tf_op jit(solution)/shard_map/collect/all_to_all | solution.py:17
  179.3 0.1 convert_reduce_fusion
  179.4 0.1 reshape.64
  179.5 0.9 fusion.6
  180.5 9.4 %all-to-all-start.3 = ((bf16[16,4,1536]{2,1,0:T(4,128)(2,1)}), bf16[16,4,1536]{2,1,0:T(4,128)(2,1)S(1)}, u32[]{:S(2)}, u32[]{:S(2)}) async-start(bf16[16,4,1536]{2,1,0:T(4,128)(2,1)} %bitcast.22), calls=%async_computation.3 | async-start | bytes 393216 | tf_op jit(solution)/shard_map/collect/all_to_all | solution.py:17
  189.9 16.0 %all-to-all-done.3 = bf16[16,4,1536]{2,1,0:T(4,128)(2,1)S(1)} async-done(((bf16[16,4,1536]{2,1,0:T(4,128)(2,1)}), bf16[16,4,1536]{2,1,0:T(4,128)(2,1)S(1)}, u32[]{:S(2)}, u32[]{:S(2)}) %all-to-all-start.3) | async-done | bytes 196640 | tf_op jit(solution)/shard_map/collect/all_to_all | solution.py:17
  205.9 0.1 convert_reduce_fusion.1
  206.0 0.1 reshape.68
  206.2 2.1 add_convert_fusion
  (57 shorter events, 0.8 us)
Async XLA Ops:
  6.5 3.2 %copy-start = (bf16[128,6144]{1,0:T(8,128)(2,1)S(1)}, bf16[128,6144]{1,0:T(8,128)(2,1)}, u32[]{:S(2)}) copy-start(bf16[128,6144]{1,0:T(8,128)(2,1)} %param.7) | copy-start | bytes 4718596
  6.5 54.7 %all-gather.4.cloned.1.call-start = ((), (), s32[]{:S(2)}) async-start(), calls=%async_computation.4 | async-start | bytes 1966080 | tf_op jit(solution)/shard_map/all_gather | solution.py:41
  7.9 1.8 copy-start.4
  7.9 1.8 copy-start.5
  7.9 1.8 copy-start.6
  8.8 75.5 %all-gather.6.cloned.1.call-start = ((), (), s32[]{:S(2)}) async-start(), calls=%async_computation.5 | async-start | bytes 1966080 | tf_op jit(solution)/shard_map/all_gather | solution.py:41
  9.6 144.1 %all-gather.8.cloned.1.call-start = ((), (), s32[]{:S(2)}) async-start(), calls=%async_computation.6 | async-start | bytes 1966080 | tf_op jit(solution)/shard_map/all_gather | solution.py:44
  57.1 4.2 %collective-permute-start = (bf16[4,64,1536]{2,1,0:T(8,128)(2,1)S(1)}, bf16[4,64,1536]{2,1,0:T(8,128)(2,1)S(1)}, u32[]{:S(2)}, u32[]{:S(2)}) collective-permute-start(bf16[4,64,1536]{2,1,0:T(8,128)(2,1)S(1)} %bitcast.64), channel_id=1, source_target_pairs={{0,1},{1,0},{2,3},{3,2},{4,5},{5,4},{6,7},{7,6},{8,9},{9,8},{10,11... | collective-permute-start | bytes 2359304 | tf_op jit(solution)/shard_map/spread_rows/ppermute | solution.py:65
  61.3 7.8 %copy-start.2 = (bf16[1536,512]{1,0:T(8,128)(2,1)S(1)}, bf16[1536,512]{1,0:T(8,128)(2,1)}, u32[]{:S(2)}) copy-start(bf16[1536,512]{1,0:T(8,128)(2,1)} %all-gather.4.cloned.1.call-done) | copy-start | bytes 4718596
  63.8 38.1 %collective-permute-start.1 = (bf16[128,512]{1,0:T(8,128)(2,1)}, bf16[128,512]{1,0:T(8,128)(2,1)S(1)}, u32[]{:S(2)}, u32[]{:S(2)}) collective-permute-start(bf16[128,512]{1,0:T(8,128)(2,1)} %convolution_convert_fusion.6), channel_id=1, source_target_pairs={{0,64},{32,96},{64,0},{96,32},{1,65},{33,97},{65,1},{97,33},{2,66}... | collective-permute-start | bytes 393224 | tf_op jit(solution)/shard_map/expert/ppermute | solution.py:25
  70.1 38.7 %collective-permute-start.2 = (bf16[128,512]{1,0:T(8,128)(2,1)}, bf16[128,512]{1,0:T(8,128)(2,1)S(1)}, u32[]{:S(2)}, u32[]{:S(2)}) collective-permute-start(bf16[128,512]{1,0:T(8,128)(2,1)} %convolution_convert_fusion.5), channel_id=1, source_target_pairs={{0,32},{32,64},{64,96},{96,0},{1,33},{33,65},{65,97},{97,1},{2,34}... | collective-permute-start | bytes 393224 | tf_op jit(solution)/shard_map/expert/ppermute | solution.py:25
  77.3 31.5 %collective-permute-start.3 = (bf16[128,512]{1,0:T(8,128)(2,1)}, bf16[128,512]{1,0:T(8,128)(2,1)S(1)}, u32[]{:S(2)}, u32[]{:S(2)}) collective-permute-start(bf16[128,512]{1,0:T(8,128)(2,1)} %convolution_convert_fusion.4), channel_id=1, source_target_pairs={{0,96},{32,0},{64,32},{96,64},{1,97},{33,1},{65,33},{97,65},{2,98}... | collective-permute-start | bytes 393224 | tf_op jit(solution)/shard_map/expert/ppermute | solution.py:25
  84.3 13.8 %copy-start.1 = (bf16[1536,512]{1,0:T(8,128)(2,1)S(1)}, bf16[1536,512]{1,0:T(8,128)(2,1)}, u32[]{:S(2)}) copy-start(bf16[1536,512]{1,0:T(8,128)(2,1)} %all-gather.6.cloned.1.call-done) | copy-start | bytes 4718596
  86.2 33.3 %collective-permute-start.7 = (bf16[128,512]{1,0:T(8,128)(2,1)S(1)}, bf16[128,512]{1,0:T(8,128)(2,1)S(1)}, u32[]{:S(2)}, u32[]{:S(2)}) collective-permute-start(bf16[128,512]{1,0:T(8,128)(2,1)S(1)} %convolution_convert_fusion.3), channel_id=1, source_target_pairs={{0,64},{32,96},{64,0},{96,32},{1,65},{33,97},{65,1},{97,33},{2,66}... | collective-permute-start | bytes 393224 | tf_op jit(solution)/shard_map/expert/ppermute | solution.py:25
  98.5 10.3 %copy-start.3 = (bf16[1536,512]{1,0:T(8,128)(2,1)S(1)}, bf16[1536,512]{1,0:T(8,128)(2,1)}, u32[]{:S(2)}) copy-start(bf16[1536,512]{1,0:T(8,128)(2,1)} %all-gather.4.cloned.1.call-done) | copy-start | bytes 4718596
  98.5 23.3 %collective-permute-start.8 = (bf16[128,512]{1,0:T(8,128)(2,1)S(1)}, bf16[128,512]{1,0:T(8,128)(2,1)S(1)}, u32[]{:S(2)}, u32[]{:S(2)}) collective-permute-start(bf16[128,512]{1,0:T(8,128)(2,1)S(1)} %convolution_convert_fusion.2), channel_id=1, source_target_pairs={{0,32},{32,64},{64,96},{96,0},{1,33},{33,65},{65,97},{97,1},{2,34}... | collective-permute-start | bytes 393224 | tf_op jit(solution)/shard_map/expert/ppermute | solution.py:25
  101.9 19.9 %collective-permute-start.9 = (bf16[128,512]{1,0:T(8,128)(2,1)S(1)}, bf16[128,512]{1,0:T(8,128)(2,1)S(1)}, u32[]{:S(2)}, u32[]{:S(2)}) collective-permute-start(bf16[128,512]{1,0:T(8,128)(2,1)S(1)} %convolution_convert_fusion.1), channel_id=1, source_target_pairs={{0,96},{32,0},{64,32},{96,64},{1,97},{33,1},{65,33},{97,65},{2,98}... | collective-permute-start | bytes 393224 | tf_op jit(solution)/shard_map/expert/ppermute | solution.py:25
  109.3 27.9 %collective-permute-start.4 = (bf16[128,256]{1,0:T(8,128)(2,1)S(1)}, bf16[128,256]{1,0:T(8,128)(2,1)S(1)}, u32[]{:S(2)}, u32[]{:S(2)}) collective-permute-start(bf16[128,256]{1,0:T(8,128)(2,1)S(1)} %fusion.16), channel_id=1, source_target_pairs={{0,96},{32,0},{64,32},{96,64},{1,97},{33,1},{65,33},{97,65},{2,98}... | collective-permute-start | bytes 196616 | tf_op jit(solution)/shard_map/expert/ppermute | solution.py:25
  112.3 31.7 %collective-permute-start.5 = (bf16[128,256]{1,0:T(8,128)(2,1)S(1)}, bf16[128,256]{1,0:T(8,128)(2,1)S(1)}, u32[]{:S(2)}, u32[]{:S(2)}) collective-permute-start(bf16[128,256]{1,0:T(8,128)(2,1)S(1)} %fusion.16), channel_id=1, source_target_pairs={{0,64},{32,96},{64,0},{96,32},{1,65},{33,97},{65,1},{97,33},{2,66}... | collective-permute-start | bytes 196616 | tf_op jit(solution)/shard_map/expert/ppermute | solution.py:25
  119.5 24.5 %collective-permute-start.6 = (bf16[128,256]{1,0:T(8,128)(2,1)S(1)}, bf16[128,256]{1,0:T(8,128)(2,1)S(1)}, u32[]{:S(2)}, u32[]{:S(2)}) collective-permute-start(bf16[128,256]{1,0:T(8,128)(2,1)S(1)} %fusion.16), channel_id=1, source_target_pairs={{0,32},{32,64},{64,96},{96,0},{1,33},{33,65},{65,97},{97,1},{2,34}... | collective-permute-start | bytes 196616 | tf_op jit(solution)/shard_map/expert/ppermute | solution.py:25
  122.3 21.8 %collective-permute-start.10 = (bf16[128,256]{1,0:T(8,128)(2,1)S(1)}, bf16[128,256]{1,0:T(8,128)(2,1)S(1)}, u32[]{:S(2)}, u32[]{:S(2)}) collective-permute-start(bf16[128,256]{1,0:T(8,128)(2,1)S(1)} %fusion.15), channel_id=1, source_target_pairs={{0,96},{32,0},{64,32},{96,64},{1,97},{33,1},{65,33},{97,65},{2,98}... | collective-permute-start | bytes 196616 | tf_op jit(solution)/shard_map/expert/ppermute | solution.py:25
  129.8 16.1 %collective-permute-start.11 = (bf16[128,256]{1,0:T(8,128)(2,1)S(1)}, bf16[128,256]{1,0:T(8,128)(2,1)S(1)}, u32[]{:S(2)}, u32[]{:S(2)}) collective-permute-start(bf16[128,256]{1,0:T(8,128)(2,1)S(1)} %fusion.15), channel_id=1, source_target_pairs={{0,64},{32,96},{64,0},{96,32},{1,65},{33,97},{65,1},{97,33},{2,66}... | collective-permute-start | bytes 196616 | tf_op jit(solution)/shard_map/expert/ppermute | solution.py:25
  137.2 16.4 %collective-permute-start.12 = (bf16[128,256]{1,0:T(8,128)(2,1)S(1)}, bf16[128,256]{1,0:T(8,128)(2,1)S(1)}, u32[]{:S(2)}, u32[]{:S(2)}) collective-permute-start(bf16[128,256]{1,0:T(8,128)(2,1)S(1)} %fusion.15), channel_id=1, source_target_pairs={{0,32},{32,64},{64,96},{96,0},{1,33},{33,65},{65,97},{97,1},{2,34}... | collective-permute-start | bytes 196616 | tf_op jit(solution)/shard_map/expert/ppermute | solution.py:25
  156.2 5.3 %collective-permute-start.13 = (f32[256,1536]{1,0:T(8,128)S(1)}, f32[256,1536]{1,0:T(8,128)S(1)}, u32[]{:S(2)}, u32[]{:S(2)}) collective-permute-start(f32[256,1536]{1,0:T(8,128)S(1)} %slice.91), channel_id=1, source_target_pairs={{0,1},{1,0},{2,3},{3,2},{4,5},{5,4},{6,7},{7,6},{8,9},{9,8},{10,11... | collective-permute-start | bytes 4718600 | tf_op jit(solution)/shard_map/collect/ppermute | solution.py:108
  162.6 16.7 %all-to-all-start.2 = ((bf16[4,64,1536]{2,1,0:T(8,128)(2,1)}), bf16[4,64,1536]{2,1,0:T(8,128)(2,1)S(1)}, u32[]{:S(2)}, u32[]{:S(2)}) async-start(bf16[4,64,1536]{2,1,0:T(8,128)(2,1)} %bitcast.21), calls=%async_computation.2 | async-start | bytes 1572864 | tf_op jit(solution)/shard_map/collect/all_to_all | solution.py:17
  180.5 25.4 %all-to-all-start.3 = ((bf16[16,4,1536]{2,1,0:T(4,128)(2,1)}), bf16[16,4,1536]{2,1,0:T(4,128)(2,1)S(1)}, u32[]{:S(2)}, u32[]{:S(2)}) async-start(bf16[16,4,1536]{2,1,0:T(4,128)(2,1)} %bitcast.22), calls=%async_computation.3 | async-start | bytes 393216 | tf_op jit(solution)/shard_map/collect/all_to_all | solution.py:17
Sparse Core Ops, SparseCore 0:
  9.5 38.3 all-gather.3
  49.9 34.3 all-gather.5
  86.4 34.3 all-gather.7

commit v3 on v2

--- a/solution.py
+++ b/solution.py
@@ -7,9 +7,8 @@
 SLOT_DEV = 4
 AXES = ("y", "zh", "zl", "x", "c")
 SIZES = (4, 4, 4, 4, 2)
-CHUNKS = 2
-AG = "pp"
-XC = False
+PARTS = (512,)
+SUMS, SPREADS = ("pp",), ("a2a",)
 BF16, F32 = jnp.bfloat16, jnp.float32
 
 
@@ -31,16 +30,13 @@
     piece = d // (ny * ns)
     cols = ny * piece
     ff = w_gate.shape[1]
-    part = ff // CHUNKS
     swap = [(0, 1), (1, 0)]
 
-    stacked = []
-    for k in range(CHUNKS):
-        stacked += [w_gate[:, k * part : (k + 1) * part], w_up[:, k * part : (k + 1) * part]]
-    in_rows = [
-        lax.all_gather(jnp.concatenate(stacked[2 * k : 2 * k + 2], axis=1), "y", axis=0, tiled=True)
-        for k in range(CHUNKS)
-    ]
+    in_rows, at = [], 0
+    for part in PARTS:
+        own = jnp.concatenate([w_gate[:, at : at + part], w_up[:, at : at + part]], axis=1)
+        in_rows.append(lax.all_gather(own, "y", axis=0, tiled=True))
+        at += part
     down_cols = lax.all_gather(w_down, "y", axis=1, tiled=True)
 
     slot_base = lax.axis_index(("zl", "x", "c")) * SLOT_DEV
@@ -73,44 +69,47 @@
 
         order = sorted(range(1, ns), key=lambda k: -min(k, ns - k))
         gathered = []
-        for h in range(CHUNKS):
+        for h, part in enumerate(PARTS):
 
             def product(k):
                 picked = lax.dynamic_index_in_dim(block, (zh + k) % ns, 0, keepdims=False)
                 return jnp.dot(picked, in_rows[h], preferred_element_type=F32)
 
-            arrived = [send(product(k).astype(BF16), "zh", ns, k) for k in order]
-            both = product(0)
-            for term in arrived:
-                both = both + term.astype(F32)
+            if SUMS[h] == "pp":
+                far = product(2).astype(BF16)
+                mid = many // 2
+                above = send(far[:mid], "zh", ns, 1).astype(F32)
+                below = send(far[mid:], "zh", ns, -1).astype(F32)
+                ahead, back = product(1), product(ns - 1)
+                ahead = jnp.concatenate([ahead[:mid] + above, ahead[mid:]], axis=0)
+                back = jnp.concatenate([back[:mid], back[mid:] + below], axis=0)
+                ahead = send(ahead.astype(BF16), "zh", ns, 1)
+                back = send(back.astype(BF16), "zh", ns, -1)
+                both = product(0) + ahead.astype(F32) + back.astype(F32)
+            else:
+                both = jnp.dot(
+                    block.reshape(ns * many, cols), in_rows[h], preferred_element_type=F32
+                )
+                both = exchange(both.astype(BF16).reshape(ns, many, 2 * part), "zh")
+                both = jnp.sum(both.astype(F32), axis=0)
             hidden = (jax.nn.silu(both[:, :part]) * both[:, part:]).astype(BF16)
-            if AG == "pp":
+            if SPREADS[h] == "pp":
                 got = {k: send(hidden, "zh", ns, -k) for k in order}
                 got[0] = hidden
-                gathered.append(jnp.stack([got[k] for k in range(ns)]))
+                turned = jnp.stack([got[k] for k in [*range(ns), *range(ns - 1)]])
+                gathered.append(lax.dynamic_slice_in_dim(turned, (ns - zh) % ns, ns, 0))
             else:
-                gathered.append(hidden)
+                gathered.append(spread(hidden, "zh", ns))
         hidden = jnp.concatenate(gathered, axis=-1)
-        if AG != "pp":
-            hidden = spread(hidden, "zh", ns)
         hidden = jnp.transpose(hidden.reshape(ns, nc, nx, few, ff), (1, 2, 0, 3, 4))
         total = jnp.dot(hidden.reshape(ns * many, ff), down_cols, preferred_element_type=F32)
 
     with jax.named_scope("collect"):
-        if XC:
-            mine = lax.axis_index("c")
-            terms = total.reshape(nx, 2, ns * few, cols)
-            terms = jnp.where(mine == 0, terms, terms[:, ::-1])
-            terms = terms.astype(BF16).reshape(nx * 2, ns * few, cols)
-            terms = exchange(terms, ("x", "c"))
-        else:
-            terms = total.reshape(nc, nx * ns * few, cols)
-            terms = terms[0] + lax.ppermute(terms[1], "c", swap)
-            terms = exchange(terms.astype(BF16).reshape(nx, ns * few, cols), "x")
+        terms = total.reshape(nc, nx * ns * few, cols)
+        terms = terms[0] + lax.ppermute(terms[1], "c", swap)
+        terms = exchange(terms.astype(BF16).reshape(nx, ns * few, cols), "x")
         terms = jnp.sum(terms.astype(F32), axis=0)
         terms = terms.reshape(ns, nl, SLOT_DEV, cols)
-        terms = jnp.concatenate([terms, terms[:-1]], axis=0)
-        terms = lax.dynamic_slice_in_dim(terms, (ns - zh) % ns, ns, 0)
         terms = terms.astype(BF16).reshape(ns * nl, SLOT_DEV, cols)
         terms = exchange(terms, ("zh", "zl")).astype(F32)
         terms = jnp.sum(terms.reshape(ns, nl, SLOT_DEV, cols), axis=1)

time: 216 us -> 213 us (0.986)
  starting transfers between devices: 88.3 us -> 33.6 us
  blocking collectives: 46.7 us -> 90.5 us
  waiting for transfers between devices: 47.1 us -> 56.9 us
    ppermute x12 -> x4, starting transfers between devices: 70.8 us -> 18.4 us  [send(): lax.ppermute(block, axis, [(i, (i + steps) % size) for i in range(size)])]
    all_to_all x2 -> x4, blocking collectives: 46.7 us -> 90.5 us  [exchange(): return lax.all_to_all(pieces, axis, 0, 0, tiled=True)]
    ppermute x12 -> x4, waiting for transfers between devices: 9.56 us -> 35.7 us  [send(): lax.ppermute(block, axis, [(i, (i + steps) % size) for i in range(size)])]
    all_to_all x2 -> x1, waiting for transfers between devices: 28.6 us -> 15.5 us  [exchange(): return lax.all_to_all(pieces, axis, 0, 0, tiled=True)]
    all_gather x2 -> x1, waiting for transfers between devices: 3.4 us -> 0.01 us  [per_device(): in_rows.append(lax.all_gather(own, 'y', axis=0, tiled=True))]
    all_to_all x2 -> x1, starting transfers between devices: 13.6 us -> 11.3 us  [exchange(): return lax.all_to_all(pieces, axis, 0, 0, tiled=True)]
    dot_general x8 -> x4, matrix products: 8.06 us -> 6.33 us  [product(): return jnp.dot(picked, in_rows[h], preferred_element_type=F32)]
  transfers between devices with their start and end apart: 19 -> 9, of which waited for: 7 -> 7; matrix products, arithmetic and copies ran while one was open for 5% -> 3% of each run, Pallas kernels for 0% -> 0%
where the time goes in v3:
time: 213 us
  blocking collectives  90.5 us (42%)
  waiting for transfers between devices  56.9 us (27%)
  starting transfers between devices  33.6 us (16%)
  between operations  13.8 us (6%)
  matrix products  9.03 us (4%)
  other arithmetic  7.75 us (4%)
    all_to_all x4, blocking collectives, exchange(): return lax.all_to_all(pieces, axis, 0, 0, tiled=True)  90.5 us
    ppermute x4, waiting for transfers between devices, send(): lax.ppermute(block, axis, [(i, (i + steps) % size) for i in range(size)])  35.7 us
    ppermute x4, starting transfers between devices, send(): lax.ppermute(block, axis, [(i, (i + steps) % size) for i in range(size)])  18.4 us
    all_to_all x1, waiting for transfers between devices, exchange(): return lax.all_to_all(pieces, axis, 0, 0, tiled=True)  15.5 us
    all_to_all x1, starting transfers between devices, exchange(): return lax.all_to_all(pieces, axis, 0, 0, tiled=True)  11.3 us
    dot_general x4, matrix products, product(): return jnp.dot(picked, in_rows[h], preferred_element_type=F32)  6.33 us
  transfers between devices with their start and end apart: 9, of which 7 were waited for; matrix products, arithmetic and copies ran while one was open for 3% of the time, Pallas kernels for 0%

profile of v3, /device:TPU:32, one launch (start us, length us, event | category | flops | bytes accessed | tf_op | source)
XLA Modules:
  0.0 212.9 jit_solution(17842190027105921067)
XLA Ops:
  6.5 0.0 copy-start
  6.5 0.0 all-gather.3.cloned.1.call-start
  6.5 2.2 %pad_maximum_fusion = bf16[384,1024]{1,0:T(8,128)(2,1)} fusion(bf16[384,512]{1,0:T(8,128)(2,1)} %param.12, bf16[384,512]{1,0:T(8,128)(2,1)} %param.11), kind=kLoop, calls=%fused_computation.15 | loop fusion | flops 1572864 | bytes 1572864 | tf_op jit(solution)/shard_map/concatenate | solution.py:37
  8.7 0.0 all-gather.3.cloned.1.call-update
  8.8 0.0 all-gather.5.cloned.1.call-start
  8.8 0.7 compare_select_fusion
  9.5 0.7 select_reduce_fusion
  10.2 0.0 copy-done
  10.2 0.3 convolution_convert_fusion
  10.6 0.1 broadcast_in_dim.29
  10.7 30.8 %all_to_all.25 = bf16[16,4,1536]{2,1,0:T(4,128)(2,1)S(1)} all-to-all(bf16[16,4,1536]{2,1,0:T(4,128)(2,1)S(1)} %bitcast.54), channel_id=1, replica_groups=mesh['y'=4,'zh'=4,'zl'=4,'x'=4,'c'=2] {'zh','zl'}, dimensions={0} | all-to-all | bytes 393216 | tf_op jit(solution)/shard_map/spread_rows/all_to_all | solution.py:16
  41.5 0.1 broadcast_in_dim.30
  41.6 0.1 broadcast_in_dim.31
  41.6 15.9 %all_to_all.26 = bf16[4,64,1536]{2,1,0:T(8,128)(2,1)S(1)} all-to-all(bf16[4,64,1536]{2,1,0:T(8,128)(2,1)S(1)} %broadcast_in_dim.31), channel_id=1, replica_groups=mesh['y'=4,'zh'=4,'zl'=4,'x'=4,'c'=2] {'x'}, dimensions={0} | all-to-all | bytes 1572864 | tf_op jit(solution)/shard_map/spread_rows/all_to_all | solution.py:16
  57.5 0.1 copy.23
  57.6 1.9 collective-permute-start
  59.5 2.2 %collective-permute-done = bf16[4,64,1536]{2,1,0:T(8,128)(2,1)S(1)} collective-permute-done((bf16[4,64,1536]{2,1,0:T(8,128)(2,1)S(1)}, bf16[4,64,1536]{2,1,0:T(8,128)(2,1)S(1)}, u32[]{:S(2)}, u32[]{:S(2)}) %collective-permute-start) | collective-permute-done | bytes 786464 | tf_op jit(solution)/shard_map/spread_rows/ppermute | solution.py:61
  61.8 2.6 %convolution_convert_fusion.1 = bf16[128,1024]{1,0:T(8,128)(2,1)S(1)} fusion(bf16[1536,1024]{1,0:T(8,128)(2,1)} %all-gather.3.cloned.1.call-done, s32[]{:T(128)S(6)} %select_n.42, bf16[4,64,1536]{2,1,0:T(8,128)(2,1)S(1)} %bitcast.46, bf16[4,64,1536]{2,1,0:T(8,128)(2,1)S(1)} %collective-permute-done), kind=kOutput, calls=%fused_computation.14 | convolution fusion | flops 403570688 | bytes 4980740 | tf_op jit(solution)/shard_map/expert/dot_general | solution.py:76
  64.4 6.7 %collective-permute-start.1 = (bf16[64,1024]{1,0:T(8,128)(2,1)S(1)}, bf16[64,1024]{1,0:T(8,128)(2,1)S(1)}, u32[]{:S(2)}, u32[]{:S(2)}) collective-permute-start(bf16[64,1024]{1,0:T(8,128)(2,1)S(1)} %get-tuple-element.7), channel_id=1, source_target_pairs={{0,32},{32,64},{64,96},{96,0},{1,33},{33,65},{65,97},{97,1},{2,34}... | collective-permute-start | bytes 393224 | tf_op jit(solution)/shard_map/expert/ppermute | solution.py:24
  71.2 0.6 fusion.11
  71.8 3.0 %collective-permute-start.3 = (bf16[64,1024]{1,0:T(8,128)(2,1)S(1)}, bf16[64,1024]{1,0:T(8,128)(2,1)S(1)}, u32[]{:S(2)}, u32[]{:S(2)}) collective-permute-start(bf16[64,1024]{1,0:T(8,128)(2,1)S(1)} %get-tuple-element.8), channel_id=1, source_target_pairs={{0,96},{32,0},{64,32},{96,64},{1,97},{33,1},{65,33},{97,65},{2,98}... | collective-permute-start | bytes 393224 | tf_op jit(solution)/shard_map/expert/ppermute | solution.py:24
  74.8 0.6 fusion.4
  75.4 6.4 %collective-permute-done.1 = bf16[64,1024]{1,0:T(8,128)(2,1)S(1)} collective-permute-done((bf16[64,1024]{1,0:T(8,128)(2,1)S(1)}, bf16[64,1024]{1,0:T(8,128)(2,1)S(1)}, u32[]{:S(2)}, u32[]{:S(2)}) %collective-permute-start.1) | collective-permute-done | bytes 131104 | tf_op jit(solution)/shard_map/expert/ppermute | solution.py:24
  81.9 0.7 pad_maximum_fusion.1
  82.6 5.5 %collective-permute-start.2 = (bf16[128,1024]{1,0:T(8,128)(2,1)}, bf16[128,1024]{1,0:T(8,128)(2,1)S(1)}, u32[]{:S(2)}, u32[]{:S(2)}) collective-permute-start(bf16[128,1024]{1,0:T(8,128)(2,1)} %pad_maximum_fusion.1), channel_id=1, source_target_pairs={{0,32},{32,64},{64,96},{96,0},{1,33},{33,65},{65,97},{97,1},{2,34}... | collective-permute-start | bytes 786440 | tf_op jit(solution)/shard_map/expert/ppermute | solution.py:24
  88.1 2.2 %collective-permute-done.3 = bf16[64,1024]{1,0:T(8,128)(2,1)S(1)} collective-permute-done((bf16[64,1024]{1,0:T(8,128)(2,1)S(1)}, bf16[64,1024]{1,0:T(8,128)(2,1)S(1)}, u32[]{:S(2)}, u32[]{:S(2)}) %collective-permute-start.3) | collective-permute-done | bytes 131104 | tf_op jit(solution)/shard_map/expert/ppermute | solution.py:24
  90.4 0.7 pad_maximum_fusion.2
  91.1 3.1 %collective-permute-start.4 = (bf16[128,1024]{1,0:T(8,128)(2,1)}, bf16[128,1024]{1,0:T(8,128)(2,1)}, u32[]{:S(2)}, u32[]{:S(2)}) collective-permute-start(bf16[128,1024]{1,0:T(8,128)(2,1)} %pad_maximum_fusion.2), channel_id=1, source_target_pairs={{0,96},{32,0},{64,32},{96,64},{1,97},{33,1},{65,33},{97,65},{2,98}... | collective-permute-start | bytes 786440 | tf_op jit(solution)/shard_map/expert/ppermute | solution.py:24
  94.3 0.0 all-gather.5.cloned.1.call-update
  94.3 3.6 %collective-permute-done.2 = bf16[128,1024]{1,0:T(8,128)(2,1)S(1)} collective-permute-done((bf16[128,1024]{1,0:T(8,128)(2,1)}, bf16[128,1024]{1,0:T(8,128)(2,1)S(1)}, u32[]{:S(2)}, u32[]{:S(2)}) %collective-permute-start.2) | collective-permute-done | bytes 262176 | tf_op jit(solution)/shard_map/expert/ppermute | solution.py:24
  97.9 23.5 %collective-permute-done.4 = bf16[128,1024]{1,0:T(8,128)(2,1)} collective-permute-done((bf16[128,1024]{1,0:T(8,128)(2,1)}, bf16[128,1024]{1,0:T(8,128)(2,1)}, u32[]{:S(2)}, u32[]{:S(2)}) %collective-permute-start.4) | collective-permute-done | bytes 262176 | tf_op jit(solution)/shard_map/expert/ppermute | solution.py:24
  121.4 2.5 %fusion.1 = f32[128,1024]{1,0:T(8,128)S(1)} fusion(bf16[1536,1024]{1,0:T(8,128)(2,1)} %all-gather.3.cloned.1.call-done, bf16[128,1024]{1,0:T(8,128)(2,1)} %collective-permute-done.4, bf16[128,1024]{1,0:T(8,128)(2,1)S(1)} %collective-permute-done.2, s32[]{:T(128)S(6)} %select_n.38, bf16[4,64,1536]{2,1,0:T(8,128)(2,1)S(1)} %bitcast.49, ...), kind=kOutput, calls=%fused_computation.13 | convolution fusion | flops 403963904 | bytes 5767172 | tf_op jit(solution)/shard_map/expert/dot_general | solution.py:76
  123.9 0.1 fusion.16
  124.1 28.5 %all_to_all.27 = bf16[4,128,512]{2,1,0:T(8,128)(2,1)S(1)} all-to-all(bf16[4,128,512]{2,1,0:T(8,128)(2,1)S(1)} %broadcast_in_dim.32), channel_id=1, replica_groups=mesh['y'=4,'zh'=4,'zl'=4,'x'=4,'c'=2] {'zh'}, dimensions={0} | all-to-all | bytes 1048576 | tf_op jit(solution)/shard_map/expert/all_to_all | solution.py:16
  152.6 0.0 all-gather.5.cloned.1.call-done
  152.6 2.4 %fusion.30 = f32[512,1536]{1,0:T(8,128)S(1)} fusion(bf16[512,512]{1,0:T(8,128)(2,1)S(1)} %bitcast.52, bf16[512,1536]{1,0:T(8,128)(2,1)} %all-gather.5.cloned.1.call-done), kind=kOutput, calls=%fused_computation.57 | convolution fusion | flops 805306368 | bytes 5242880 | tf_op jit(solution)/shard_map/expert/dot_general | solution.py:105
  155.0 0.1 slice.89
  155.1 1.9 collective-permute-start.5
  157.1 3.4 %collective-permute-done.5 = f32[256,1536]{1,0:T(8,128)S(1)} collective-permute-done((f32[256,1536]{1,0:T(8,128)S(1)}, f32[256,1536]{1,0:T(8,128)S(1)}, u32[]{:S(2)}, u32[]{:S(2)}) %collective-permute-start.5) | collective-permute-done | bytes 1572896 | tf_op jit(solution)/shard_map/collect/ppermute | solution.py:109
  160.4 0.2 fusion
  160.7 15.3 %all_to_all.28 = bf16[4,64,1536]{2,1,0:T(8,128)(2,1)S(1)} all-to-all(bf16[4,64,1536]{2,1,0:T(8,128)(2,1)S(1)} %bitcast.51), channel_id=1, replica_groups=mesh['y'=4,'zh'=4,'zl'=4,'x'=4,'c'=2] {'x'}, dimensions={0} | all-to-all | bytes 1572864 | tf_op jit(solution)/shard_map/collect/all_to_all | solution.py:16
  176.0 0.1 reduce_sum.41
  176.1 0.7 convert_element_type.52
  176.8 11.3 %all-to-all-start.4 = ((bf16[16,4,1536]{2,1,0:T(4,128)(2,1)}), bf16[16,4,1536]{2,1,0:T(4,128)(2,1)S(1)}, u32[]{:S(2)}, u32[]{:S(2)}) async-start(bf16[16,4,1536]{2,1,0:T(4,128)(2,1)} %convert_element_type.52), calls=%async_computation.4 | async-start | bytes 393216 | tf_op jit(solution)/shard_map/collect/all_to_all | solution.py:16
  188.1 15.5 %all-to-all-done.4 = bf16[16,4,1536]{2,1,0:T(4,128)(2,1)S(1)} async-done(((bf16[16,4,1536]{2,1,0:T(4,128)(2,1)}), bf16[16,4,1536]{2,1,0:T(4,128)(2,1)S(1)}, u32[]{:S(2)}, u32[]{:S(2)}) %all-to-all-start.4) | async-done | bytes 196640 | tf_op jit(solution)/shard_map/collect/all_to_all | solution.py:16
  203.6 0.1 convert_reduce_fusion
  203.7 0.1 reshape.64
  203.9 2.1 %add_convert_fusion = bf16[128,6144]{1,0:T(8,128)(2,1)} fusion(f32[6144]{0:T(1024)S(1)} %mul.116, f32[128]{0:T(128)S(1)} %get-tuple-element.14, f32[6144]{0:T(1024)S(1)} %mul.111, f32[128]{0:T(128)S(1)} %get-tuple-element.15, f32[6144]{0:T(1024)S(1)} %mul.106, f32[128]{0:T(128)S(1)} %get-tuple-element.16, f32[6144]{0:T(1024)S(1)} %mul.101, ...), kind=kLoop, calls=%fused_computation.1 | loop fusion | flops 6291456 | bytes 1673216 | tf_op jit(solution)/shard_map/convert_element_type | solution.py:123
  (23 shorter events, 0.4 us)
Async XLA Ops:
  6.5 3.7 %copy-start = (bf16[128,6144]{1,0:T(8,128)(2,1)S(1)}, bf16[128,6144]{1,0:T(8,128)(2,1)}, u32[]{:S(2)}) copy-start(bf16[128,6144]{1,0:T(8,128)(2,1)} %param.7) | copy-start | bytes 4718596
  6.5 55.2 %all-gather.3.cloned.1.call-start = ((), (), s32[]{:S(2)}) async-start(), calls=%async_computation.5 | async-start | bytes 3932160 | tf_op jit(solution)/shard_map/all_gather | solution.py:38
  8.8 143.9 %all-gather.5.cloned.1.call-start = ((), (), s32[]{:S(2)}) async-start(), calls=%async_computation.6 | async-start | bytes 1966080 | tf_op jit(solution)/shard_map/all_gather | solution.py:40
  57.6 4.2 %collective-permute-start = (bf16[4,64,1536]{2,1,0:T(8,128)(2,1)S(1)}, bf16[4,64,1536]{2,1,0:T(8,128)(2,1)S(1)}, u32[]{:S(2)}, u32[]{:S(2)}) collective-permute-start(bf16[4,64,1536]{2,1,0:T(8,128)(2,1)S(1)} %bitcast.45), channel_id=1, source_target_pairs={{0,1},{1,0},{2,3},{3,2},{4,5},{5,4},{6,7},{7,6},{8,9},{9,8},{10,11... | collective-permute-start | bytes 2359304 | tf_op jit(solution)/shard_map/spread_rows/ppermute | solution.py:61
  61.8 9.4 %copy-start.1 = (bf16[1536,1024]{1,0:T(8,128)(2,1)S(1)}, bf16[1536,1024]{1,0:T(8,128)(2,1)}, u32[]{:S(2)}) copy-start(bf16[1536,1024]{1,0:T(8,128)(2,1)} %all-gather.3.cloned.1.call-done) | copy-start | bytes 9437188
  64.4 17.4 %collective-permute-start.1 = (bf16[64,1024]{1,0:T(8,128)(2,1)S(1)}, bf16[64,1024]{1,0:T(8,128)(2,1)S(1)}, u32[]{:S(2)}, u32[]{:S(2)}) collective-permute-start(bf16[64,1024]{1,0:T(8,128)(2,1)S(1)} %get-tuple-element.7), channel_id=1, source_target_pairs={{0,32},{32,64},{64,96},{96,0},{1,33},{33,65},{65,97},{97,1},{2,34}... | collective-permute-start | bytes 393224 | tf_op jit(solution)/shard_map/expert/ppermute | solution.py:24
  71.8 18.6 %collective-permute-start.3 = (bf16[64,1024]{1,0:T(8,128)(2,1)S(1)}, bf16[64,1024]{1,0:T(8,128)(2,1)S(1)}, u32[]{:S(2)}, u32[]{:S(2)}) collective-permute-start(bf16[64,1024]{1,0:T(8,128)(2,1)S(1)} %get-tuple-element.8), channel_id=1, source_target_pairs={{0,96},{32,0},{64,32},{96,64},{1,97},{33,1},{65,33},{97,65},{2,98}... | collective-permute-start | bytes 393224 | tf_op jit(solution)/shard_map/expert/ppermute | solution.py:24
  82.6 15.3 %collective-permute-start.2 = (bf16[128,1024]{1,0:T(8,128)(2,1)}, bf16[128,1024]{1,0:T(8,128)(2,1)S(1)}, u32[]{:S(2)}, u32[]{:S(2)}) collective-permute-start(bf16[128,1024]{1,0:T(8,128)(2,1)} %pad_maximum_fusion.1), channel_id=1, source_target_pairs={{0,32},{32,64},{64,96},{96,0},{1,33},{33,65},{65,97},{97,1},{2,34}... | collective-permute-start | bytes 786440 | tf_op jit(solution)/shard_map/expert/ppermute | solution.py:24
  91.1 30.3 %collective-permute-start.4 = (bf16[128,1024]{1,0:T(8,128)(2,1)}, bf16[128,1024]{1,0:T(8,128)(2,1)}, u32[]{:S(2)}, u32[]{:S(2)}) collective-permute-start(bf16[128,1024]{1,0:T(8,128)(2,1)} %pad_maximum_fusion.2), channel_id=1, source_target_pairs={{0,96},{32,0},{64,32},{96,64},{1,97},{33,1},{65,33},{97,65},{2,98}... | collective-permute-start | bytes 786440 | tf_op jit(solution)/shard_map/expert/ppermute | solution.py:24
  155.1 5.3 %collective-permute-start.5 = (f32[256,1536]{1,0:T(8,128)S(1)}, f32[256,1536]{1,0:T(8,128)S(1)}, u32[]{:S(2)}, u32[]{:S(2)}) collective-permute-start(f32[256,1536]{1,0:T(8,128)S(1)} %slice.89), channel_id=1, source_target_pairs={{0,1},{1,0},{2,3},{3,2},{4,5},{5,4},{6,7},{7,6},{8,9},{9,8},{10,11... | collective-permute-start | bytes 4718600 | tf_op jit(solution)/shard_map/collect/ppermute | solution.py:109
  176.8 26.8 %all-to-all-start.4 = ((bf16[16,4,1536]{2,1,0:T(4,128)(2,1)}), bf16[16,4,1536]{2,1,0:T(4,128)(2,1)S(1)}, u32[]{:S(2)}, u32[]{:S(2)}) async-start(bf16[16,4,1536]{2,1,0:T(4,128)(2,1)} %convert_element_type.52), calls=%async_computation.4 | async-start | bytes 393216 | tf_op jit(solution)/shard_map/collect/all_to_all | solution.py:16
Sparse Core Ops, SparseCore 0:
  9.5 51.3 all-gather.2
  94.4 34.0 all-gather.4
